TPU v7x, 256 devices: a whole 4x4x8 slice. The times are simulated.
256 devices in a mesh: dp: 16 (over x, y), tensor: 16 (over z, core).
Axes of the slice: x: 4, y: 4, z: 8, core: 2. Of those that a mesh axis runs over, the one named last changes fastest.
Arguments:
- activations: bfloat16 [4096, 16384], P('dp', 'tensor'), may hold values from -6 to 6
- angles: float32 [14, 8192], P(None, 'tensor'), may hold values from -3.140625 to 3.140625
- clip_bits: int32 [256, 16384], P('dp', 'tensor'), may hold values from 0 to 65535, as said below
- codes: bfloat16 [16384, 10240], P('tensor', 'dp'), may hold values from -127 to 127, as said below
- exponents: int32 [10240], replicated, may hold values from -16 to -13
- cotangent: bfloat16 [4096, 10240], P('dp', 'tensor'), may hold values from -6 to 6
Outputs:
- input_grad: bfloat16 [4096, 16384], P('dp', 'tensor')
- angle_grad: float32 [14, 8192], P(None, 'tensor')
Inputs may be any that keep to these rules, and one draw needn't show every extreme that they name: Bit k (0 to 15) of clip_bits[w, i] is the clip mask of token 16 w + k at feature i; higher bits are zero. `codes`: every entry is a whole number.
All inputs are finite; a program needn't handle non-finite values.
Results may differ from a plain program's by a relative error of at most 0.003.
Values may be sent and summed in bfloat16 or wider, within the bound.
A program may use at most 128 MiB of HBM per device.

v0:
```python
import jax
import jax.numpy as jnp
from jax import lax
from jax.sharding import PartitionSpec as P


def partner(value, axis, apart):
    mask = 2**apart
    pairs = [(source, source ^ mask) for source in range(lax.axis_size(axis))]
    return lax.ppermute(value, axis, pairs)


def split_up(value, dim, count):
    shape = value.shape
    parts = value.reshape(*shape[:dim], count, shape[dim] // count, *shape[dim + 1 :])
    return jnp.moveaxis(parts, dim, 0)


def sent_and_summed(value, axis, dim):
    count = lax.axis_size(axis)
    parts = lax.all_to_all(split_up(value, dim, count), axis, 0, 0, tiled=True)
    return jnp.sum(parts, axis=0)


def copy_for_each(value, axis):
    copies = jnp.broadcast_to(value, (lax.axis_size(axis), *value.shape))
    return lax.all_to_all(copies, axis, split_axis=0, concat_axis=0, tiled=True)


def over_copies(value, axis):
    everything = copy_for_each(value, axis)
    return jnp.sum(everything, axis=0)


def unpack_mask(clip_bits, rows, width):
    shifts = jnp.arange(16, dtype=jnp.int32)
    bits = jnp.bitwise_and(jnp.right_shift(clip_bits[:, None, :], shifts[None, :, None]), 1)
    return bits.reshape(rows, width).astype(jnp.float32)


def section_terms(table, section, first, width):
    half = 1 << section
    index = first + jnp.arange(width, dtype=jnp.int32)
    pair = jnp.right_shift(index, section + 1) * half + jnp.bitwise_and(index, half - 1)
    theta = jnp.take(table[section], pair)
    lower = jnp.bitwise_and(index, half) == 0
    sign = jnp.where(lower, -1.0, 1.0).astype(jnp.float32)
    return (jnp.cos(theta), sign * jnp.sin(theta), sign, pair)


def local_partner(field, section):
    half = 1 << section
    column = jnp.arange(field.shape[1], dtype=jnp.int32)
    lower = jnp.bitwise_and(column, half) == 0
    return jnp.where(lower[None, :], jnp.roll(field, -half, axis=1), jnp.roll(field, half, axis=1))


def scatter_terms(term, pair, half_pairs):
    return jnp.zeros((half_pairs,), jnp.float32).at[pair].add(term)


def body(activations, angles, clip_bits, codes, exponents, cotangent):
    rows, width = activations.shape
    sections = angles.shape[0]
    share = angles.shape[1]
    half_pairs = share * lax.axis_size("tensor")
    local_count = width.bit_length() - 1
    place = lax.axis_index("tensor")
    table = lax.all_gather(angles, "tensor", axis=1, tiled=True)
    scale = jnp.exp2(exponents.astype(jnp.float32))
    full_cot = lax.all_gather(cotangent, "tensor", axis=1, tiled=True)
    weight_piece = (
        lax.all_gather(codes, "dp", axis=1, tiled=True).astype(jnp.float32) * scale[None, :]
    ).astype(jnp.bfloat16)
    projected = lax.dot_general(
        full_cot, weight_piece, (((1,), (1,)), ((), ())), preferred_element_type=jnp.float32
    )
    grad_rot = projected * unpack_mask(clip_bits, rows, width)
    first = place * width
    field = activations.astype(jnp.float32)
    stored = [None] * sections
    for section in range(sections):
        cosine, signed, sign, pair = section_terms(table, section, first, width)
        if section < local_count:
            other = local_partner(field, section)
        else:
            other = partner(field.astype(jnp.bfloat16), "tensor", section - local_count).astype(
                field.dtype
            )
            stored[section] = (field, other)
        field = cosine * field + signed * other
    grad = grad_rot
    terms_list = [None] * sections
    for section in reversed(range(sections)):
        cosine, signed, sign, pair = section_terms(table, section, first, width)
        if section < local_count:
            other = local_partner(field, section)
            grad_other = local_partner(grad, section)
            before = cosine * field - signed * other
        else:
            before, before_other = stored[section]
            other = cosine * before_other - signed * before
            grad_other = partner(grad, "tensor", section - local_count)
        terms_list[section] = scatter_terms(jnp.sum(sign * grad * other, axis=0), pair, half_pairs)
        grad = cosine * grad - signed * grad_other
        field = before
    input_grad = grad.astype(jnp.bfloat16)
    collected = jnp.stack(terms_list)
    partial_total = sent_and_summed(collected, "tensor", 1)
    angle_grad = over_copies(partial_total, "dp")
    return (input_grad, angle_grad)


def solution(mesh):
    placed = (
        P("dp", "tensor"),
        P(None, "tensor"),
        P("dp", "tensor"),
        P("tensor", "dp"),
        P(),
        P("dp", "tensor"),
    )
    return jax.shard_map(
        body,
        mesh=mesh,
        in_specs=placed,
        out_specs=(P("dp", "tensor"), P(None, "tensor")),
        check_vma=False,
    )
```

profile of v0, /device:TPU:1, one launch (start us, length us, event | category | flops | bytes accessed | tf_op | source)
XLA Modules:
  0.0 559.8 jit_solution(14048898341933507902)
XLA Ops:
  8.7 1.2 copy.21
  9.9 24.0 %all_gather.9 = f32[14,8192]{1,0:T(8,128)S(1)} all-gather(f32[14,512]{1,0:T(8,128)} %param.9), channel_id=1, replica_groups=mesh['dp'=16,'tensor'=16] {'tensor'}, dimensions={1}, use_global_device_ids=true | all-gather | bytes 487424 | tf_op jit(solution)/shard_map/all_gather | solution.py:69
  34.3 6.2 %gather_fusion = f32[1024]{0:T(1024)S(1)} fusion(f32[8192]{0:T(1024)S(1)} %bitcast.62, s32[1024]{0:T(1024)S(1)} %get-tuple-element.213), kind=kCustom, calls=%fused_computation.clone | custom fusion | bytes 12288 | tf_op jit(solution)/shard_map/jit(_take)/gather | solution.py:45
  40.5 6.2 %gather_fusion.1 = f32[1024]{0:T(1024)S(1)} fusion(f32[8192]{0:T(1024)S(1)} %bitcast.61, s32[1024]{0:T(1024)S(1)} %get-tuple-element.226), kind=kCustom, calls=%fused_computation.1.clone | custom fusion | bytes 12288 | tf_op jit(solution)/shard_map/jit(_take)/gather | solution.py:45
  46.7 6.2 %gather_fusion.2 = f32[1024]{0:T(1024)S(1)} fusion(f32[8192]{0:T(1024)S(1)} %bitcast.60, s32[1024]{0:T(1024)S(1)} %get-tuple-element.214), kind=kCustom, calls=%fused_computation.2.clone | custom fusion | bytes 12288 | tf_op jit(solution)/shard_map/jit(_take)/gather | solution.py:45
  52.8 6.2 %gather_fusion.3 = f32[1024]{0:T(1024)S(1)} fusion(f32[8192]{0:T(1024)S(1)} %bitcast.59, s32[1024]{0:T(1024)S(1)} %get-tuple-element.215), kind=kCustom, calls=%fused_computation.3.clone | custom fusion | bytes 12288 | tf_op jit(solution)/shard_map/jit(_take)/gather | solution.py:45
  59.0 6.2 %gather_fusion.4 = f32[1024]{0:T(1024)S(1)} fusion(f32[8192]{0:T(1024)S(1)} %bitcast.58, s32[1024]{0:T(1024)S(1)} %get-tuple-element.216), kind=kCustom, calls=%fused_computation.4.clone | custom fusion | bytes 12288 | tf_op jit(solution)/shard_map/jit(_take)/gather | solution.py:45
  65.2 6.2 %gather_fusion.5 = f32[1024]{0:T(1024)S(1)} fusion(f32[8192]{0:T(1024)S(1)} %bitcast.57, s32[1024]{0:T(1024)S(1)} %get-tuple-element.217), kind=kCustom, calls=%fused_computation.5.clone | custom fusion | bytes 12288 | tf_op jit(solution)/shard_map/jit(_take)/gather | solution.py:45
  71.3 6.2 %gather_fusion.6 = f32[1024]{0:T(1024)S(1)} fusion(f32[8192]{0:T(1024)S(1)} %bitcast.56, s32[1024]{0:T(1024)S(1)} %get-tuple-element.218), kind=kCustom, calls=%fused_computation.6.clone | custom fusion | bytes 12288 | tf_op jit(solution)/shard_map/jit(_take)/gather | solution.py:45
  77.5 6.2 %gather_fusion.7 = f32[1024]{0:T(1024)S(1)} fusion(f32[8192]{0:T(1024)S(1)} %bitcast.55, s32[1024]{0:T(1024)S(1)} %get-tuple-element.219), kind=kCustom, calls=%fused_computation.7.clone | custom fusion | bytes 12288 | tf_op jit(solution)/shard_map/jit(_take)/gather | solution.py:45
  83.7 6.2 %gather_fusion.8 = f32[1024]{0:T(1024)S(1)} fusion(f32[8192]{0:T(1024)S(1)} %bitcast.54, s32[1024]{0:T(1024)S(1)} %get-tuple-element.220), kind=kCustom, calls=%fused_computation.8.clone | custom fusion | bytes 12288 | tf_op jit(solution)/shard_map/jit(_take)/gather | solution.py:45
  89.9 6.2 %gather_fusion.9 = f32[1024]{0:T(1024)S(1)} fusion(f32[8192]{0:T(1024)S(1)} %bitcast.53, s32[1024]{0:T(1024)S(1)} %get-tuple-element.221), kind=kCustom, calls=%fused_computation.9.clone | custom fusion | bytes 12288 | tf_op jit(solution)/shard_map/jit(_take)/gather | solution.py:45
  109.1 6.1 %gather_fusion.10 = f32[1024]{0:T(1024)S(1)} fusion(f32[8192]{0:T(1024)S(1)} %bitcast.52, s32[1024]{0:T(1024)S(1)} %get-tuple-element.222), kind=kCustom, calls=%fused_computation.10.clone | custom fusion | bytes 12288 | tf_op jit(solution)/shard_map/jit(_take)/gather | solution.py:45
  115.3 6.2 %gather_fusion.11 = f32[1024]{0:T(1024)S(1)} fusion(f32[8192]{0:T(1024)S(1)} %bitcast.51, s32[1024]{0:T(1024)S(1)} %get-tuple-element.223), kind=kCustom, calls=%fused_computation.11.clone | custom fusion | bytes 12288 | tf_op jit(solution)/shard_map/jit(_take)/gather | solution.py:45
  122.9 1.3 copy.20
  124.3 11.9 %collective-permute-done.5 = bf16[256,1024]{0,1:T(8,128)(2,1)S(1)} collective-permute-done((bf16[256,1024]{0,1:T(8,128)(2,1)}, bf16[256,1024]{0,1:T(8,128)(2,1)S(1)}, u32[]{:S(2)}, u32[]{:S(2)}) %collective-permute-start.5) | collective-permute-done | bytes 524320 | tf_op jit(solution)/shard_map/ppermute | solution.py:10
  136.2 1.6 fusion.183
  137.7 58.5 %all-gather.3.cloned.1.call-done = bf16[1024,10240]{1,0:T(8,128)(2,1)} async-done(((bf16[1024,640]{1,0:T(8,128)(2,1)}), bf16[1024,10240]{1,0:T(8,128)(2,1)}) %all-gather.3.cloned.1.call-update) | async-done | bytes 20971536 | tf_op jit(solution)/shard_map/all_gather | solution.py:73
  196.2 12.5 %fusion.3 = f32[256,1024]{0,1:T(8,128)} fusion(bf16[256,10240]{1,0:T(8,128)(2,1)} %all-gather.5.cloned.1.call-done, bf16[1024,10240]{1,0:T(8,128)(2,1)} %all-gather.3.cloned.1.call-done, f32[10240]{0:T(1024)S(1)} %multiply_exponential_fusion, s32[256,1024]{0,1:T(8,128)} %copy.20, s32[256]{0:T(256)S(1)} %shift_right_arithmetic.224), kind=kOutput, calls=%fused_computation.32 | convolution fusion | flops 5401214976 | bytes 28353536 | tf_op jit(solution)/shard_map/dot_general | solution.py:75
  208.7 5.5 collective-permute-start
  214.2 6.1 %gather_fusion.12 = f32[1024]{0:T(1024)S(1)} fusion(f32[8192]{0:T(1024)S(1)} %bitcast.50, s32[1024]{0:T(1024)S(1)} %get-tuple-element.224), kind=kCustom, calls=%fused_computation.12.clone | custom fusion | bytes 12288 | tf_op jit(solution)/shard_map/jit(_take)/gather | solution.py:45
  220.4 2.2 fusion.57
  222.6 6.1 %gather_fusion.13 = f32[1024]{0:T(1024)S(1)} fusion(f32[8192]{0:T(1024)S(1)} %bitcast.49, s32[1024]{0:T(1024)S(1)} %get-tuple-element.225), kind=kCustom, calls=%fused_computation.13.clone | custom fusion | bytes 12288 | tf_op jit(solution)/shard_map/jit(_take)/gather | solution.py:45
  228.8 41.5 %collective-permute-done.7 = bf16[256,1024]{0,1:T(8,128)(2,1)} collective-permute-done((bf16[256,1024]{0,1:T(8,128)(2,1)}, bf16[256,1024]{0,1:T(8,128)(2,1)}, u32[]{:S(2)}, u32[]{:S(2)}) %collective-permute-start.7) | collective-permute-done | bytes 524320 | tf_op jit(solution)/shard_map/ppermute | solution.py:10
  270.3 2.7 multiply_reduce_fusion
  273.1 15.1 %collective-permute-start.1 = (f32[256,1024]{0,1:T(8,128)S(1)}, f32[256,1024]{0,1:T(8,128)S(1)}, u32[]{:S(2)}, u32[]{:S(2)}) collective-permute-start(f32[256,1024]{0,1:T(8,128)S(1)} %get-tuple-element.17), channel_id=1, source_target_pairs={{0,4},{1,5},{2,6},{3,7},{4,0},{5,1},{6,2},{7,3},{8,12},{9,13},{10,... | collective-permute-start | bytes 3145736 | tf_op jit(solution)/shard_map/ppermute | solution.py:10
  288.2 46.0 %collective-permute-done.1 = f32[256,1024]{0,1:T(8,128)S(1)} collective-permute-done((f32[256,1024]{0,1:T(8,128)S(1)}, f32[256,1024]{0,1:T(8,128)S(1)}, u32[]{:S(2)}, u32[]{:S(2)}) %collective-permute-start.1) | collective-permute-done | bytes 1048608 | tf_op jit(solution)/shard_map/ppermute | solution.py:10
  336.5 22.4 %collective-permute-done.2 = f32[256,1024]{0,1:T(8,128)S(1)} collective-permute-done((f32[256,1024]{0,1:T(8,128)S(1)}, f32[256,1024]{0,1:T(8,128)S(1)}, u32[]{:S(2)}, u32[]{:S(2)}) %collective-permute-start.2) | collective-permute-done | bytes 1048608 | tf_op jit(solution)/shard_map/ppermute | solution.py:10
  358.9 2.1 fusion.10
  361.0 1.3 collective-permute-start.3
  364.9 7.7 %scatter_custom_fusion.13 = f32[8192]{0:T(1024)S(1)} fusion(s32[1024]{0:T(1024)S(1)} %bitcast.91, f32[1024]{0:T(1024)S(1)} %get-tuple-element.13, f32[]{:T(128)} %constant.42.clone.1), kind=kCustom, calls=%fused_computation.161 | custom fusion | flops 1024 | bytes 32772 | tf_op jit(solution)/shard_map/scatter-add | solution.py:59
  372.6 7.7 %scatter_custom_fusion.12 = f32[8192]{0:T(1024)S(1)} fusion(s32[1024]{0:T(1024)S(1)} %bitcast.89, f32[1024]{0:T(1024)S(1)} %get-tuple-element.14, f32[]{:T(128)} %constant.42.clone.1), kind=kCustom, calls=%fused_computation.163 | custom fusion | flops 1024 | bytes 32772 | tf_op jit(solution)/shard_map/scatter-add | solution.py:59
  380.3 7.7 %scatter_custom_fusion.11 = f32[8192]{0:T(1024)S(1)} fusion(s32[1024]{0:T(1024)S(1)} %bitcast.90, f32[1024]{0:T(1024)S(1)} %get-tuple-element.15, f32[]{:T(128)} %constant.42.clone.1), kind=kCustom, calls=%fused_computation.165 | custom fusion | flops 1024 | bytes 32772 | tf_op jit(solution)/shard_map/scatter-add | solution.py:59
  387.9 7.8 %scatter_custom_fusion.10 = f32[8192]{0:T(1024)S(1)} fusion(s32[1024]{0:T(1024)S(1)} %bitcast.88, f32[1024]{0:T(1024)S(1)} %get-tuple-element.16, f32[]{:T(128)} %constant.42.clone.1), kind=kCustom, calls=%fused_computation.167 | custom fusion | flops 1024 | bytes 32772 | tf_op jit(solution)/shard_map/scatter-add | solution.py:59
  395.8 2.4 multiply_reduce_fusion.1
  398.4 1.8 multiply_reduce_fusion.2
  401.8 1.7 multiply_reduce_fusion.3
  405.0 1.6 multiply_reduce_fusion.4
  408.0 1.6 multiply_reduce_fusion.5
  411.0 1.5 multiply_reduce_fusion.6
  413.9 1.4 multiply_reduce_fusion.7
  416.9 1.5 multiply_reduce_fusion.8
  418.8 1.4 multiply_subtract_fusion
  422.0 1.6 multiply_reduce_fusion.9
  424.2 1.4 fusion.198
  425.7 7.8 %scatter_custom_fusion.9 = f32[8192]{0:T(1024)S(1)} fusion(s32[1024]{0:T(1024)} %bitcast.79, f32[1024]{0:T(1024)S(1)} %get-tuple-element.23, f32[]{:T(128)} %constant.42.clone.1), kind=kCustom, calls=%fused_computation.169 | custom fusion | flops 1024 | bytes 33280 | tf_op jit(solution)/shard_map/scatter-add | solution.py:59
  433.5 7.8 %scatter_custom_fusion.8 = f32[8192]{0:T(1024)S(1)} fusion(s32[1024]{0:T(1024)} %bitcast.87, f32[1024]{0:T(1024)S(1)} %get-tuple-element.25, f32[]{:T(128)} %constant.42.clone.1), kind=kCustom, calls=%fused_computation.171 | custom fusion | flops 1024 | bytes 33280 | tf_op jit(solution)/shard_map/scatter-add | solution.py:59
  441.3 7.8 %scatter_custom_fusion.7 = f32[8192]{0:T(1024)S(1)} fusion(s32[1024]{0:T(1024)} %bitcast.86, f32[1024]{0:T(1024)S(1)} %get-tuple-element.27, f32[]{:T(128)} %constant.42.clone.1), kind=kCustom, calls=%fused_computation.173 | custom fusion | flops 1024 | bytes 33280 | tf_op jit(solution)/shard_map/scatter-add | solution.py:59
  449.1 7.8 %scatter_custom_fusion.6 = f32[8192]{0:T(1024)S(1)} fusion(s32[1024]{0:T(1024)} %bitcast.81, f32[1024]{0:T(1024)S(1)} %get-tuple-element.29, f32[]{:T(128)} %constant.42.clone.1), kind=kCustom, calls=%fused_computation.175 | custom fusion | flops 1024 | bytes 33280 | tf_op jit(solution)/shard_map/scatter-add | solution.py:59
  456.9 7.8 %scatter_custom_fusion.5 = f32[8192]{0:T(1024)S(1)} fusion(s32[1024]{0:T(1024)} %bitcast.80, f32[1024]{0:T(1024)S(1)} %get-tuple-element.31, f32[]{:T(128)} %constant.42.clone.1), kind=kCustom, calls=%fused_computation.177 | custom fusion | flops 1024 | bytes 33280 | tf_op jit(solution)/shard_map/scatter-add | solution.py:59
  464.7 7.8 %scatter_custom_fusion.4 = f32[8192]{0:T(1024)S(1)} fusion(s32[1024]{0:T(1024)} %bitcast.83, f32[1024]{0:T(1024)S(1)} %get-tuple-element.33, f32[]{:T(128)} %constant.42.clone.1), kind=kCustom, calls=%fused_computation.179 | custom fusion | flops 1024 | bytes 33280 | tf_op jit(solution)/shard_map/scatter-add | solution.py:59
  472.5 7.8 %scatter_custom_fusion.3 = f32[8192]{0:T(1024)S(1)} fusion(s32[1024]{0:T(1024)} %bitcast.82, f32[1024]{0:T(1024)S(1)} %get-tuple-element.35, f32[]{:T(128)} %constant.42.clone.1), kind=kCustom, calls=%fused_computation.181 | custom fusion | flops 1024 | bytes 33280 | tf_op jit(solution)/shard_map/scatter-add | solution.py:59
  480.3 7.8 %scatter_custom_fusion.2 = f32[8192]{0:T(1024)S(1)} fusion(s32[1024]{0:T(1024)} %bitcast.85, f32[1024]{0:T(1024)S(1)} %get-tuple-element.37, f32[]{:T(128)} %constant.42.clone.1), kind=kCustom, calls=%fused_computation.183 | custom fusion | flops 1024 | bytes 33280 | tf_op jit(solution)/shard_map/scatter-add | solution.py:59
  488.1 8.6 %scatter_custom_fusion.1 = f32[8192]{0:T(1024)} fusion(s32[1024]{0:T(1024)} %bitcast.84, f32[1024]{0:T(1024)S(1)} %get-tuple-element.39, f32[]{:T(128)} %constant.42.clone.1), kind=kCustom, calls=%fused_computation.185 | custom fusion | flops 1024 | bytes 33280 | tf_op jit(solution)/shard_map/scatter-add | solution.py:59
  496.7 3.8 fusion.56
  500.5 7.8 %scatter_custom_fusion = f32[8192]{0:T(1024)S(1)} fusion(s32[1024]{0:T(1024)} %bitcast.78, f32[1024]{0:T(1024)} %get-tuple-element.41, f32[]{:T(128)} %constant.42.clone.1), kind=kCustom, calls=%fused_computation.187 | custom fusion | flops 1024 | bytes 33280 | tf_op jit(solution)/shard_map/scatter-add | solution.py:59
  508.3 2.8 stack.59
  511.1 4.1 all-to-all-start
  515.4 17.1 %all-to-all-done = f32[16,14,512]{2,1,0:T(8,128)} async-done(((f32[16,14,512]{2,1,0:T(8,128)}), f32[16,14,512]{2,1,0:T(8,128)}, u32[]{:S(2)}, u32[]{:S(2)}) %all-to-all-start) | async-done | bytes 458784 | tf_op jit(solution)/shard_map/all_to_all | solution.py:21
  534.5 5.0 all-to-all-start.1
  539.5 2.7 fusion.35
  542.2 2.0 copy.23
  544.2 6.6 %all-to-all-done.1 = f32[16,14,512]{2,1,0:T(8,128)} async-done(((f32[16,14,512]{2,1,0:T(8,128)}), f32[16,14,512]{2,1,0:T(8,128)}, u32[]{:S(2)}, u32[]{:S(2)}) %all-to-all-start.1) | async-done | bytes 458784 | tf_op jit(solution)/shard_map/all_to_all | solution.py:27
  550.9 1.7 reduce_sum.159
  (145 shorter events, 34.8 us)
Async XLA Ops:
  7.2 130.6 %all-gather.5.cloned.1.call-start = ((), (), s32[]{:S(2)}) async-start(), calls=%async_computation.3 | async-start | bytes 5570560 | tf_op jit(solution)/shard_map/all_gather | solution.py:71
  7.9 188.3 %all-gather.3.cloned.1.call-start = ((), (), s32[]{:S(2)}) async-start(), calls=%async_computation.2 | async-start | bytes 22282240 | tf_op jit(solution)/shard_map/all_gather | solution.py:73
  96.0 7.1 %copy-start.3 = (pred[1024]{0:T(1024)(128)(4,1)}, pred[1024]{0:T(1024)(128)(4,1)S(1)}, u32[]{:S(2)}) copy-start(pred[1024]{0:T(1024)(128)(4,1)S(1)} %and_compare_fusion) | copy-start | bytes 3076
  96.1 325.9 %copy-start.2 = (pred[1024]{0:T(1024)(128)(4,1)}, pred[1024]{0:T(1024)(128)(4,1)S(1)}, u32[]{:S(2)}) copy-start(pred[1024]{0:T(1024)(128)(4,1)S(1)} %get-tuple-element.245) | copy-start | bytes 3076
  104.2 18.6 %copy-start = (s32[16,1024]{1,0:T(8,128)S(1)}, s32[16,1024]{1,0:T(8,128)}, u32[]{:S(2)}) copy-start(s32[16,1024]{1,0:T(8,128)} %param.10) | copy-start | bytes 196612
  104.4 19.9 %copy-start.1 = (s32[10240]{0:T(1024)S(1)}, s32[10240]{0:T(1024)}, u32[]{:S(2)}) copy-start(s32[10240]{0:T(1024)} %param.12) | copy-start | bytes 122884
  108.6 13.0 %collective-permute-start.4 = (bf16[256,1024]{0,1:T(8,128)(2,1)S(1)}, bf16[256,1024]{0,1:T(8,128)(2,1)S(1)}, u32[]{:S(2)}, u32[]{:S(2)}) collective-permute-start(bf16[256,1024]{0,1:T(8,128)(2,1)S(1)} %get-tuple-element.21), channel_id=1, source_target_pairs={{0,1},{1,0},{2,3},{3,2},{4,5},{5,4},{6,7},{7,6},{8,9},{9,8},{10,11... | collective-permute-start | bytes 1572872 | tf_op jit(solution)/shard_map/ppermute | solution.py:10
  122.7 13.5 %collective-permute-start.5 = (bf16[256,1024]{0,1:T(8,128)(2,1)}, bf16[256,1024]{0,1:T(8,128)(2,1)S(1)}, u32[]{:S(2)}, u32[]{:S(2)}) collective-permute-start(bf16[256,1024]{0,1:T(8,128)(2,1)} %fusion.182), channel_id=1, source_target_pairs={{0,2},{1,3},{2,0},{3,1},{4,6},{5,7},{6,4},{7,5},{8,10},{9,11},{10,... | collective-permute-start | bytes 1572872 | tf_op jit(solution)/shard_map/ppermute | solution.py:10
  137.7 82.7 %collective-permute-start.6 = (bf16[256,1024]{0,1:T(8,128)(2,1)}, bf16[256,1024]{0,1:T(8,128)(2,1)}, u32[]{:S(2)}, u32[]{:S(2)}) collective-permute-start(bf16[256,1024]{0,1:T(8,128)(2,1)} %get-tuple-element.18), channel_id=1, source_target_pairs={{0,4},{1,5},{2,6},{3,7},{4,0},{5,1},{6,2},{7,3},{8,12},{9,13},{10,... | collective-permute-start | bytes 1572872 | tf_op jit(solution)/shard_map/ppermute | solution.py:10
  208.7 61.6 %collective-permute-start = (f32[256,1024]{0,1:T(8,128)}, f32[256,1024]{0,1:T(8,128)}, u32[]{:S(2)}, u32[]{:S(2)}) collective-permute-start(f32[256,1024]{0,1:T(8,128)} %fusion.3), channel_id=1, source_target_pairs={{0,8},{1,9},{2,10},{3,11},{4,12},{5,13},{6,14},{7,15},{8,0},{9,1},... | collective-permute-start | bytes 3145736 | tf_op jit(solution)/shard_map/ppermute | solution.py:10
  222.6 47.7 %collective-permute-start.7 = (bf16[256,1024]{0,1:T(8,128)(2,1)}, bf16[256,1024]{0,1:T(8,128)(2,1)}, u32[]{:S(2)}, u32[]{:S(2)}) collective-permute-start(bf16[256,1024]{0,1:T(8,128)(2,1)} %fusion.57), channel_id=1, source_target_pairs={{0,8},{1,9},{2,10},{3,11},{4,12},{5,13},{6,14},{7,15},{8,0},{9,1},... | collective-permute-start | bytes 1572872 | tf_op jit(solution)/shard_map/ppermute | solution.py:10
  273.1 61.2 %collective-permute-start.1 = (f32[256,1024]{0,1:T(8,128)S(1)}, f32[256,1024]{0,1:T(8,128)S(1)}, u32[]{:S(2)}, u32[]{:S(2)}) collective-permute-start(f32[256,1024]{0,1:T(8,128)S(1)} %get-tuple-element.17), channel_id=1, source_target_pairs={{0,4},{1,5},{2,6},{3,7},{4,0},{5,1},{6,2},{7,3},{8,12},{9,13},{10,... | collective-permute-start | bytes 3145736 | tf_op jit(solution)/shard_map/ppermute | solution.py:10
  334.6 24.3 %collective-permute-start.2 = (f32[256,1024]{0,1:T(8,128)S(1)}, f32[256,1024]{0,1:T(8,128)S(1)}, u32[]{:S(2)}, u32[]{:S(2)}) collective-permute-start(f32[256,1024]{0,1:T(8,128)S(1)} %multiply_subtract_fusion.11), channel_id=1, source_target_pairs={{0,2},{1,3},{2,0},{3,1},{4,6},{5,7},{6,4},{7,5},{8,10},{9,11},{10,... | collective-permute-start | bytes 3145736 | tf_op jit(solution)/shard_map/ppermute | solution.py:10
  361.0 34.8 %collective-permute-start.3 = (f32[256,1024]{0,1:T(8,128)}, f32[256,1024]{0,1:T(8,128)S(1)}, u32[]{:S(2)}, u32[]{:S(2)}) collective-permute-start(f32[256,1024]{0,1:T(8,128)} %get-tuple-element.20), channel_id=1, source_target_pairs={{0,1},{1,0},{2,3},{3,2},{4,5},{5,4},{6,7},{7,6},{8,9},{9,8},{10,11... | collective-permute-start | bytes 3145736 | tf_op jit(solution)/shard_map/ppermute | solution.py:10
  511.1 21.4 %all-to-all-start = ((f32[16,14,512]{2,1,0:T(8,128)}), f32[16,14,512]{2,1,0:T(8,128)}, u32[]{:S(2)}, u32[]{:S(2)}) async-start(f32[16,14,512]{2,1,0:T(8,128)} %bitcast.44), calls=%async_computation | async-start | bytes 1048576 | tf_op jit(solution)/shard_map/all_to_all | solution.py:21
  534.5 16.4 %all-to-all-start.1 = ((f32[16,14,512]{2,1,0:T(8,128)}), f32[16,14,512]{2,1,0:T(8,128)}, u32[]{:S(2)}, u32[]{:S(2)}) async-start(f32[16,14,512]{2,1,0:T(8,128)} %broadcast_in_dim.368), calls=%async_computation.1 | async-start | bytes 1048576 | tf_op jit(solution)/shard_map/all_to_all | solution.py:27
Sparse Core Ops, SparseCore 0:
  9.8 48.4 all-gather.4
  60.7 135.4 all-gather.2
where the time goes:
time: 569 us; the launch traced here: 560 us
  waiting for transfers between devices  205 us (36%)
  other arithmetic  167 us (29%)
  local copies, waits for them, and re-layouts  103 us (18%)
  starting transfers between devices  31.8 us (6%)
  blocking collectives  24 us (4%)
  between operations  15.6 us (3%)
  matrix products  12.5 us (2%)
    ppermute x8, waiting for transfers between devices, partner(): return lax.ppermute(value, axis, pairs)  122 us
    scatter-add x14, other arithmetic, scatter_terms(): return jnp.zeros((half_pairs,), jnp.float32).at[pair].add(term)  110 us
    gather x14, local copies, waits for them, and re-layouts, section_terms(): theta = jnp.take(table[section], pair)  86.1 us
    all_gather x1, waiting for transfers between devices, body(): lax.all_gather(codes, 'dp', axis=1, tiled=True).astype(jnp.float32)  58.5 us
    all_gather x1, blocking collectives, body(): table = lax.all_gather(angles, 'tensor', axis=1, tiled=True)  24 us
    reduce_sum x12, other arithmetic, body(): jnp.sum(sign * grad * other, axis=0)  23.8 us
    ppermute x8, starting transfers between devices, partner(): return lax.ppermute(value, axis, pairs)  22.6 us
    all_to_all x1, waiting for transfers between devices, sent_and_summed(): parts = lax.all_to_all(split_up(value, dim, count), axis, 0, 0, tiled=True)  17.1 us
  transfers between devices with their start and end apart: 12, of which 7 were waited for; matrix products, arithmetic and copies ran while one was open for 28% of the time, Pallas kernels for 0%

commit v1 on v0

--- a/solution.py
+++ b/solution.py
@@ -2,6 +2,16 @@
 import jax.numpy as jnp
 from jax import lax
 from jax.sharding import PartitionSpec as P
+
+
+def around_the_ring(x, name, d):
+    size = lax.axis_size(name)
+    moving, pieces = (x, [x])
+    for _ in range(size - 1):
+        moving = lax.ppermute(moving, name, [(i, (i + 1) % size) for i in range(size)])
+        pieces.insert(0, moving)
+    line = jnp.concatenate(pieces, axis=d)
+    return jnp.roll(line, (lax.axis_index(name) + 1) * x.shape[d], axis=d)
 
 
 def partner(value, axis, apart):
@@ -66,7 +76,7 @@
     half_pairs = share * lax.axis_size("tensor")
     local_count = width.bit_length() - 1
     place = lax.axis_index("tensor")
-    table = lax.all_gather(angles, "tensor", axis=1, tiled=True)
+    table = around_the_ring(angles, "tensor", 1)
     scale = jnp.exp2(exponents.astype(jnp.float32))
     full_cot = lax.all_gather(cotangent, "tensor", axis=1, tiled=True)
     weight_piece = (

time: 569 us -> 562 us (0.988)
  blocking collectives: 24 us -> 0 us
  waiting for transfers between devices: 205 us -> 219 us
  starting transfers between devices: 31.8 us -> 41.3 us
    ppermute x0 -> x15, waiting for transfers between devices: none -> 62.9 us  [around_the_ring(): lax.ppermute(moving, name, [(i, (i + 1) % size) for i in range(size)])]
    all_gather x1, waiting for transfers between devices: 58.5 us -> 12.3 us  [body(): lax.all_gather(codes, 'dp', axis=1, tiled=True).astype(jnp.float32)]
    all_gather x1 -> x0, blocking collectives: 24 us -> none  [body(): table = lax.all_gather(angles, 'tensor', axis=1, tiled=True)]
    ppermute x0 -> x15, starting transfers between devices: none -> 5.89 us  [around_the_ring(): lax.ppermute(moving, name, [(i, (i + 1) % size) for i in range(size)])]
  transfers between devices with their start and end apart: 12 -> 27, of which waited for: 7 -> 22; matrix products, arithmetic and copies ran while one was open for 28% -> 29% of each run, Pallas kernels for 0% -> 0%
where the time goes in v1:
time: 562 us; the launch traced here: 558 us
  waiting for transfers between devices  219 us (39%)
  other arithmetic  164 us (29%)
  local copies, waits for them, and re-layouts  106 us (19%)
  starting transfers between devices  41.3 us (7%)
  between operations  15.9 us (3%)
  matrix products  12.5 us (2%)
    ppermute x8, waiting for transfers between devices, partner(): return lax.ppermute(value, axis, pairs)  118 us
    scatter-add x14, other arithmetic, scatter_terms(): return jnp.zeros((half_pairs,), jnp.float32).at[pair].add(term)  108 us
    gather x14, local copies, waits for them, and re-layouts, section_terms(): theta = jnp.take(table[section], pair)  86.7 us
    ppermute x15, waiting for transfers between devices, around_the_ring(): lax.ppermute(moving, name, [(i, (i + 1) % size) for i in range(size)])  62.9 us
    ppermute x8, starting transfers between devices, partner(): return lax.ppermute(value, axis, pairs)  26.2 us
    reduce_sum x12, other arithmetic, body(): jnp.sum(sign * grad * other, axis=0)  24.1 us
    all_to_all x1, waiting for transfers between devices, sent_and_summed(): parts = lax.all_to_all(split_up(value, dim, count), axis, 0, 0, tiled=True)  17.1 us
    dot_general x1, matrix products, body(): lax.dot_general(full_cot, weight_piece, (((1,), (1,)), ((), ())), preferr...  12.5 us
  transfers between devices with their start and end apart: 27, of which 22 were waited for; matrix products, arithmetic and copies ran while one was open for 29% of the time, Pallas kernels for 0%

profile of v1, /device:TPU:1, one launch (start us, length us, event | category | flops | bytes accessed | tf_op | source)
XLA Modules:
  0.0 558.4 jit_solution(839142587188800612)
XLA Ops:
  8.6 3.0 collective-permute-start
  13.0 2.2 collective-permute-start.1
  18.7 3.8 collective-permute-done.2
  22.5 4.5 collective-permute-done.3
  27.1 5.0 collective-permute-done.4
  32.1 5.0 collective-permute-done.5
  37.1 4.9 collective-permute-done.6
  42.0 4.9 collective-permute-done.7
  47.5 4.6 collective-permute-done.8
  52.1 4.8 collective-permute-done.9
  56.9 4.5 collective-permute-done.10
  61.5 4.5 collective-permute-done.11
  66.0 4.5 collective-permute-done.12
  70.6 4.5 collective-permute-done.13
  75.1 4.5 collective-permute-done.14
  82.5 6.3 %gather_fusion = f32[1024]{0:T(1024)S(1)} fusion(f32[8192]{0:T(1024)S(1)} %bitcast.62, s32[1024]{0:T(1024)S(1)} %get-tuple-element.213), kind=kCustom, calls=%fused_computation.clone | custom fusion | bytes 12288 | tf_op jit(solution)/shard_map/jit(_take)/gather | solution.py:55
  88.8 6.2 %gather_fusion.1 = f32[1024]{0:T(1024)S(1)} fusion(f32[8192]{0:T(1024)S(1)} %bitcast.61, s32[1024]{0:T(1024)S(1)} %get-tuple-element.226), kind=kCustom, calls=%fused_computation.1.clone | custom fusion | bytes 12288 | tf_op jit(solution)/shard_map/jit(_take)/gather | solution.py:55
  95.0 6.2 %gather_fusion.2 = f32[1024]{0:T(1024)S(1)} fusion(f32[8192]{0:T(1024)S(1)} %bitcast.60, s32[1024]{0:T(1024)S(1)} %get-tuple-element.214), kind=kCustom, calls=%fused_computation.2.clone | custom fusion | bytes 12288 | tf_op jit(solution)/shard_map/jit(_take)/gather | solution.py:55
  101.1 6.2 %gather_fusion.3 = f32[1024]{0:T(1024)S(1)} fusion(f32[8192]{0:T(1024)S(1)} %bitcast.59, s32[1024]{0:T(1024)S(1)} %get-tuple-element.215), kind=kCustom, calls=%fused_computation.3.clone | custom fusion | bytes 12288 | tf_op jit(solution)/shard_map/jit(_take)/gather | solution.py:55
  107.3 6.2 %gather_fusion.4 = f32[1024]{0:T(1024)S(1)} fusion(f32[8192]{0:T(1024)S(1)} %bitcast.58, s32[1024]{0:T(1024)S(1)} %get-tuple-element.216), kind=kCustom, calls=%fused_computation.4.clone | custom fusion | bytes 12288 | tf_op jit(solution)/shard_map/jit(_take)/gather | solution.py:55
  113.4 6.2 %gather_fusion.5 = f32[1024]{0:T(1024)S(1)} fusion(f32[8192]{0:T(1024)S(1)} %bitcast.57, s32[1024]{0:T(1024)S(1)} %get-tuple-element.217), kind=kCustom, calls=%fused_computation.5.clone | custom fusion | bytes 12288 | tf_op jit(solution)/shard_map/jit(_take)/gather | solution.py:55
  119.6 6.2 %gather_fusion.6 = f32[1024]{0:T(1024)S(1)} fusion(f32[8192]{0:T(1024)S(1)} %bitcast.56, s32[1024]{0:T(1024)S(1)} %get-tuple-element.218), kind=kCustom, calls=%fused_computation.6.clone | custom fusion | bytes 12288 | tf_op jit(solution)/shard_map/jit(_take)/gather | solution.py:55
  125.8 6.2 %gather_fusion.7 = f32[1024]{0:T(1024)S(1)} fusion(f32[8192]{0:T(1024)S(1)} %bitcast.55, s32[1024]{0:T(1024)S(1)} %get-tuple-element.219), kind=kCustom, calls=%fused_computation.7.clone | custom fusion | bytes 12288 | tf_op jit(solution)/shard_map/jit(_take)/gather | solution.py:55
  131.9 6.2 %gather_fusion.8 = f32[1024]{0:T(1024)S(1)} fusion(f32[8192]{0:T(1024)S(1)} %bitcast.54, s32[1024]{0:T(1024)S(1)} %get-tuple-element.220), kind=kCustom, calls=%fused_computation.8.clone | custom fusion | bytes 12288 | tf_op jit(solution)/shard_map/jit(_take)/gather | solution.py:55
  138.1 6.2 %gather_fusion.9 = f32[1024]{0:T(1024)S(1)} fusion(f32[8192]{0:T(1024)S(1)} %bitcast.53, s32[1024]{0:T(1024)S(1)} %get-tuple-element.221), kind=kCustom, calls=%fused_computation.9.clone | custom fusion | bytes 12288 | tf_op jit(solution)/shard_map/jit(_take)/gather | solution.py:55
  156.6 3.9 collective-permute-start.19
  162.1 6.6 %gather_fusion.10 = f32[1024]{0:T(1024)S(1)} fusion(f32[8192]{0:T(1024)S(1)} %bitcast.52, s32[1024]{0:T(1024)S(1)} %get-tuple-element.222), kind=kCustom, calls=%fused_computation.10.clone | custom fusion | bytes 12288 | tf_op jit(solution)/shard_map/jit(_take)/gather | solution.py:55
  169.2 6.2 %gather_fusion.11 = f32[1024]{0:T(1024)S(1)} fusion(f32[8192]{0:T(1024)S(1)} %bitcast.51, s32[1024]{0:T(1024)S(1)} %get-tuple-element.223), kind=kCustom, calls=%fused_computation.11.clone | custom fusion | bytes 12288 | tf_op jit(solution)/shard_map/jit(_take)/gather | solution.py:55
  175.4 7.4 %collective-permute-done.20 = bf16[256,1024]{0,1:T(8,128)(2,1)S(1)} collective-permute-done((bf16[256,1024]{0,1:T(8,128)(2,1)S(1)}, bf16[256,1024]{0,1:T(8,128)(2,1)S(1)}, u32[]{:S(2)}, u32[]{:S(2)}) %collective-permute-start.20) | collective-permute-done | bytes 524320 | tf_op jit(solution)/shard_map/ppermute | solution.py:20
  184.5 12.3 %all-gather.3.cloned.1.call-done = bf16[1024,10240]{1,0:T(8,128)(2,1)} async-done(((bf16[1024,640]{1,0:T(8,128)(2,1)}), bf16[1024,10240]{1,0:T(8,128)(2,1)}) %all-gather.3.cloned.1.call-update) | async-done | bytes 20971536 | tf_op jit(solution)/shard_map/all_gather | solution.py:83
  196.9 12.5 %fusion.3 = f32[256,1024]{0,1:T(8,128)} fusion(bf16[256,10240]{1,0:T(8,128)(2,1)} %all-gather.5.cloned.1.call-done, bf16[1024,10240]{1,0:T(8,128)(2,1)} %all-gather.3.cloned.1.call-done, f32[10240]{0:T(1024)S(1)} %multiply_exponential_fusion, s32[256,1024]{0,1:T(8,128)} %copy.20, s32[256]{0:T(256)S(1)} %shift_right_arithmetic.224), kind=kOutput, calls=%fused_computation.32 | convolution fusion | flops 5401214976 | bytes 28353536 | tf_op jit(solution)/shard_map/dot_general | solution.py:85
  209.4 5.4 collective-permute-start.15
  214.8 6.1 %gather_fusion.12 = f32[1024]{0:T(1024)S(1)} fusion(f32[8192]{0:T(1024)S(1)} %bitcast.50, s32[1024]{0:T(1024)S(1)} %get-tuple-element.224), kind=kCustom, calls=%fused_computation.12.clone | custom fusion | bytes 12288 | tf_op jit(solution)/shard_map/jit(_take)/gather | solution.py:55
  221.0 2.2 fusion.57
  223.2 6.2 %gather_fusion.13 = f32[1024]{0:T(1024)S(1)} fusion(f32[8192]{0:T(1024)S(1)} %bitcast.49, s32[1024]{0:T(1024)S(1)} %copy-done.18), kind=kCustom, calls=%fused_computation.13.clone | custom fusion | bytes 12288 | tf_op jit(solution)/shard_map/jit(_take)/gather | solution.py:55
  229.4 41.5 %collective-permute-done.22 = bf16[256,1024]{0,1:T(8,128)(2,1)} collective-permute-done((bf16[256,1024]{0,1:T(8,128)(2,1)}, bf16[256,1024]{0,1:T(8,128)(2,1)}, u32[]{:S(2)}, u32[]{:S(2)}) %collective-permute-start.22) | collective-permute-done | bytes 524320 | tf_op jit(solution)/shard_map/ppermute | solution.py:20
  270.9 2.7 multiply_reduce_fusion
  273.7 15.1 %collective-permute-start.16 = (f32[256,1024]{0,1:T(8,128)S(1)}, f32[256,1024]{0,1:T(8,128)S(1)}, u32[]{:S(2)}, u32[]{:S(2)}) collective-permute-start(f32[256,1024]{0,1:T(8,128)S(1)} %get-tuple-element.17), channel_id=1, source_target_pairs={{0,4},{1,5},{2,6},{3,7},{4,0},{5,1},{6,2},{7,3},{8,12},{9,13},{10,... | collective-permute-start | bytes 3145736 | tf_op jit(solution)/shard_map/ppermute | solution.py:20
  288.8 46.1 %collective-permute-done.16 = f32[256,1024]{0,1:T(8,128)S(1)} collective-permute-done((f32[256,1024]{0,1:T(8,128)S(1)}, f32[256,1024]{0,1:T(8,128)S(1)}, u32[]{:S(2)}, u32[]{:S(2)}) %collective-permute-start.16) | collective-permute-done | bytes 1048608 | tf_op jit(solution)/shard_map/ppermute | solution.py:20
  336.0 23.5 %collective-permute-done.17 = f32[256,1024]{0,1:T(8,128)S(1)} collective-permute-done((f32[256,1024]{0,1:T(8,128)S(1)}, f32[256,1024]{0,1:T(8,128)S(1)}, u32[]{:S(2)}, u32[]{:S(2)}) %collective-permute-start.17) | collective-permute-done | bytes 1048608 | tf_op jit(solution)/shard_map/ppermute | solution.py:20
  359.5 2.1 fusion.10
  364.4 7.7 %scatter_custom_fusion.13 = f32[8192]{0:T(1024)S(1)} fusion(s32[1024]{0:T(1024)S(1)} %bitcast.91, f32[1024]{0:T(1024)S(1)} %get-tuple-element.13, f32[]{:T(128)} %constant.115.clone.1), kind=kCustom, calls=%fused_computation.193 | custom fusion | flops 1024 | bytes 32772 | tf_op jit(solution)/shard_map/scatter-add | solution.py:69
  372.1 7.7 %scatter_custom_fusion.12 = f32[8192]{0:T(1024)S(1)} fusion(s32[1024]{0:T(1024)S(1)} %bitcast.89, f32[1024]{0:T(1024)S(1)} %get-tuple-element.14, f32[]{:T(128)} %constant.115.clone.1), kind=kCustom, calls=%fused_computation.195 | custom fusion | flops 1024 | bytes 32772 | tf_op jit(solution)/shard_map/scatter-add | solution.py:69
  379.7 7.7 %scatter_custom_fusion.11 = f32[8192]{0:T(1024)S(1)} fusion(s32[1024]{0:T(1024)S(1)} %bitcast.90, f32[1024]{0:T(1024)S(1)} %get-tuple-element.15, f32[]{:T(128)} %constant.115.clone.1), kind=kCustom, calls=%fused_computation.197 | custom fusion | flops 1024 | bytes 32772 | tf_op jit(solution)/shard_map/scatter-add | solution.py:69
  387.4 7.7 %scatter_custom_fusion.10 = f32[8192]{0:T(1024)S(1)} fusion(s32[1024]{0:T(1024)S(1)} %bitcast.88, f32[1024]{0:T(1024)S(1)} %get-tuple-element.16, f32[]{:T(128)} %constant.115.clone.1), kind=kCustom, calls=%fused_computation.199 | custom fusion | flops 1024 | bytes 32772 | tf_op jit(solution)/shard_map/scatter-add | solution.py:69
  395.1 2.5 multiply_reduce_fusion.1
  425.4 7.7 %scatter_custom_fusion.9 = f32[8192]{0:T(1024)S(1)} fusion(s32[1024]{0:T(1024)S(1)} %bitcast.79, f32[1024]{0:T(1024)S(1)} %get-tuple-element.23, f32[]{:T(128)} %constant.115.clone.1), kind=kCustom, calls=%fused_computation.201 | custom fusion | flops 1024 | bytes 32772 | tf_op jit(solution)/shard_map/scatter-add | solution.py:69
  433.1 7.7 %scatter_custom_fusion.8 = f32[8192]{0:T(1024)S(1)} fusion(s32[1024]{0:T(1024)S(1)} %bitcast.87, f32[1024]{0:T(1024)S(1)} %get-tuple-element.25, f32[]{:T(128)} %constant.115.clone.1), kind=kCustom, calls=%fused_computation.203 | custom fusion | flops 1024 | bytes 32772 | tf_op jit(solution)/shard_map/scatter-add | solution.py:69
  440.7 7.7 %scatter_custom_fusion.7 = f32[8192]{0:T(1024)S(1)} fusion(s32[1024]{0:T(1024)S(1)} %bitcast.86, f32[1024]{0:T(1024)S(1)} %get-tuple-element.27, f32[]{:T(128)} %constant.115.clone.1), kind=kCustom, calls=%fused_computation.205 | custom fusion | flops 1024 | bytes 32772 | tf_op jit(solution)/shard_map/scatter-add | solution.py:69
  448.4 7.7 %scatter_custom_fusion.6 = f32[8192]{0:T(1024)S(1)} fusion(s32[1024]{0:T(1024)S(1)} %bitcast.81, f32[1024]{0:T(1024)S(1)} %get-tuple-element.29, f32[]{:T(128)} %constant.115.clone.1), kind=kCustom, calls=%fused_computation.207 | custom fusion | flops 1024 | bytes 32772 | tf_op jit(solution)/shard_map/scatter-add | solution.py:69
  456.1 7.7 %scatter_custom_fusion.5 = f32[8192]{0:T(1024)S(1)} fusion(s32[1024]{0:T(1024)S(1)} %bitcast.80, f32[1024]{0:T(1024)S(1)} %get-tuple-element.31, f32[]{:T(128)} %constant.115.clone.1), kind=kCustom, calls=%fused_computation.209 | custom fusion | flops 1024 | bytes 32772 | tf_op jit(solution)/shard_map/scatter-add | solution.py:69
  463.7 7.7 %scatter_custom_fusion.4 = f32[8192]{0:T(1024)S(1)} fusion(s32[1024]{0:T(1024)S(1)} %bitcast.83, f32[1024]{0:T(1024)S(1)} %get-tuple-element.33, f32[]{:T(128)} %constant.115.clone.1), kind=kCustom, calls=%fused_computation.211 | custom fusion | flops 1024 | bytes 32772 | tf_op jit(solution)/shard_map/scatter-add | solution.py:69
  471.4 7.7 %scatter_custom_fusion.3 = f32[8192]{0:T(1024)S(1)} fusion(s32[1024]{0:T(1024)S(1)} %bitcast.82, f32[1024]{0:T(1024)S(1)} %get-tuple-element.35, f32[]{:T(128)} %constant.115.clone.1), kind=kCustom, calls=%fused_computation.213 | custom fusion | flops 1024 | bytes 32772 | tf_op jit(solution)/shard_map/scatter-add | solution.py:69
  479.1 7.8 %scatter_custom_fusion.2 = f32[8192]{0:T(1024)S(1)} fusion(s32[1024]{0:T(1024)} %bitcast.85, f32[1024]{0:T(1024)S(1)} %get-tuple-element.37, f32[]{:T(128)} %constant.115.clone.1), kind=kCustom, calls=%fused_computation.215 | custom fusion | flops 1024 | bytes 33280 | tf_op jit(solution)/shard_map/scatter-add | solution.py:69
  486.9 8.6 %scatter_custom_fusion.1 = f32[8192]{0:T(1024)} fusion(s32[1024]{0:T(1024)} %bitcast.84, f32[1024]{0:T(1024)S(1)} %get-tuple-element.39, f32[]{:T(128)} %constant.115.clone.1), kind=kCustom, calls=%fused_computation.217 | custom fusion | flops 1024 | bytes 33280 | tf_op jit(solution)/shard_map/scatter-add | solution.py:69
  495.5 3.8 fusion.56
  499.3 7.8 %scatter_custom_fusion = f32[8192]{0:T(1024)S(1)} fusion(s32[1024]{0:T(1024)} %bitcast.78, f32[1024]{0:T(1024)} %get-tuple-element.41, f32[]{:T(128)} %constant.115.clone.1), kind=kCustom, calls=%fused_computation.219 | custom fusion | flops 1024 | bytes 33280 | tf_op jit(solution)/shard_map/scatter-add | solution.py:69
  507.1 2.8 stack.59
  509.9 4.1 all-to-all-start
  514.2 17.1 %all-to-all-done = f32[16,14,512]{2,1,0:T(8,128)} async-done(((f32[16,14,512]{2,1,0:T(8,128)}), f32[16,14,512]{2,1,0:T(8,128)}, u32[]{:S(2)}, u32[]{:S(2)}) %all-to-all-start) | async-done | bytes 458784 | tf_op jit(solution)/shard_map/all_to_all | solution.py:31
  533.3 5.0 all-to-all-start.1
  538.3 2.6 fusion.35
  540.9 2.0 copy.23
  543.0 6.7 %all-to-all-done.1 = f32[16,14,512]{2,1,0:T(8,128)} async-done(((f32[16,14,512]{2,1,0:T(8,128)}), f32[16,14,512]{2,1,0:T(8,128)}, u32[]{:S(2)}, u32[]{:S(2)}) %all-to-all-start.1) | async-done | bytes 458784 | tf_op jit(solution)/shard_map/all_to_all | solution.py:37
  (238 shorter events, 60.5 us)
Async XLA Ops:
  7.2 177.3 %all-gather.5.cloned.1.call-start = ((), (), s32[]{:S(2)}) async-start(), calls=%async_computation.3 | async-start | bytes 5570560 | tf_op jit(solution)/shard_map/all_gather | solution.py:81
  7.9 189.0 %all-gather.3.cloned.1.call-start = ((), (), s32[]{:S(2)}) async-start(), calls=%async_computation.2 | async-start | bytes 22282240 | tf_op jit(solution)/shard_map/all_gather | solution.py:83
  8.6 4.4 collective-permute-start
  13.0 4.9 collective-permute-start.1
  18.0 4.6 collective-permute-start.2
  22.5 4.6 collective-permute-start.3
  27.1 5.1 collective-permute-start.4
  32.1 5.0 collective-permute-start.5
  37.1 4.9 collective-permute-start.6
  42.0 4.9 collective-permute-start.7
  46.9 5.2 collective-permute-start.8
  52.1 4.8 collective-permute-start.9
  56.9 4.6 collective-permute-start.10
  56.9 96.8 %copy-start.12 = (pred[1024]{0:T(1024)(128)(4,1)}, pred[1024]{0:T(1024)(128)(4,1)S(1)}, u32[]{:S(2)}) copy-start(pred[1024]{0:T(1024)(128)(4,1)S(1)} %get-tuple-element.239) | copy-start | bytes 3076
  56.9 98.1 %copy-start.16 = (pred[1024]{0:T(1024)(128)(4,1)}, pred[1024]{0:T(1024)(128)(4,1)S(1)}, u32[]{:S(2)}) copy-start(pred[1024]{0:T(1024)(128)(4,1)S(1)} %get-tuple-element.240) | copy-start | bytes 3076
  61.5 4.6 collective-permute-start.11
  61.5 89.8 %copy-start.8 = (pred[1024]{0:T(1024)(128)(4,1)}, pred[1024]{0:T(1024)(128)(4,1)S(1)}, u32[]{:S(2)}) copy-start(pred[1024]{0:T(1024)(128)(4,1)S(1)} %get-tuple-element.241) | copy-start | bytes 3076
  61.5 91.0 %copy-start.10 = (pred[1024]{0:T(1024)(128)(4,1)}, pred[1024]{0:T(1024)(128)(4,1)S(1)}, u32[]{:S(2)}) copy-start(pred[1024]{0:T(1024)(128)(4,1)S(1)} %get-tuple-element.242) | copy-start | bytes 3076
  66.0 4.6 collective-permute-start.12
  66.0 82.8 %copy-start.4 = (pred[1024]{0:T(1024)(128)(4,1)}, pred[1024]{0:T(1024)(128)(4,1)S(1)}, u32[]{:S(2)}) copy-start(pred[1024]{0:T(1024)(128)(4,1)S(1)} %get-tuple-element.243) | copy-start | bytes 3076
  66.0 83.9 %copy-start.6 = (pred[1024]{0:T(1024)(128)(4,1)}, pred[1024]{0:T(1024)(128)(4,1)S(1)}, u32[]{:S(2)}) copy-start(pred[1024]{0:T(1024)(128)(4,1)S(1)} %get-tuple-element.244) | copy-start | bytes 3076
  70.6 4.5 collective-permute-start.13
  70.6 75.5 %copy-start.14 = (pred[1024]{0:T(1024)(128)(4,1)}, pred[1024]{0:T(1024)(128)(4,1)S(1)}, u32[]{:S(2)}) copy-start(pred[1024]{0:T(1024)(128)(4,1)S(1)} %get-tuple-element.245) | copy-start | bytes 3076
  70.6 76.9 %copy-start.2 = (pred[1024]{0:T(1024)(128)(4,1)}, pred[1024]{0:T(1024)(128)(4,1)S(1)}, u32[]{:S(2)}) copy-start(pred[1024]{0:T(1024)(128)(4,1)S(1)} %get-tuple-element.246) | copy-start | bytes 3076
  75.1 4.6 collective-permute-start.14
  75.1 69.7 %copy-start.19 = (pred[1024]{0:T(1024)(128)(4,1)}, pred[1024]{0:T(1024)(128)(4,1)S(1)}, u32[]{:S(2)}) copy-start(pred[1024]{0:T(1024)(128)(4,1)S(1)} %and_compare_fusion) | copy-start | bytes 3076
  150.0 10.7 %copy-start = (s32[16,1024]{1,0:T(8,128)S(1)}, s32[16,1024]{1,0:T(8,128)}, u32[]{:S(2)}) copy-start(s32[16,1024]{1,0:T(8,128)} %param.10) | copy-start | bytes 196612
  152.3 16.9 %copy-start.1 = (s32[10240]{0:T(1024)S(1)}, s32[10240]{0:T(1024)}, u32[]{:S(2)}) copy-start(s32[10240]{0:T(1024)} %param.12) | copy-start | bytes 122884
  156.6 12.1 %collective-permute-start.19 = (bf16[256,1024]{0,1:T(8,128)(2,1)S(1)}, bf16[256,1024]{0,1:T(8,128)(2,1)S(1)}, u32[]{:S(2)}, u32[]{:S(2)}) collective-permute-start(bf16[256,1024]{0,1:T(8,128)(2,1)S(1)} %get-tuple-element.21), channel_id=1, source_target_pairs={{0,1},{1,0},{2,3},{3,2},{4,5},{5,4},{6,7},{7,6},{8,9},{9,8},{10,11... | collective-permute-start | bytes 1572872 | tf_op jit(solution)/shard_map/ppermute | solution.py:20
  169.1 13.7 %collective-permute-start.20 = (bf16[256,1024]{0,1:T(8,128)(2,1)S(1)}, bf16[256,1024]{0,1:T(8,128)(2,1)S(1)}, u32[]{:S(2)}, u32[]{:S(2)}) collective-permute-start(bf16[256,1024]{0,1:T(8,128)(2,1)S(1)} %fusion.182), channel_id=1, source_target_pairs={{0,2},{1,3},{2,0},{3,1},{4,6},{5,7},{6,4},{7,5},{8,10},{9,11},{10,... | collective-permute-start | bytes 1572872 | tf_op jit(solution)/shard_map/ppermute | solution.py:20
  184.4 38.8 %copy-start.18 = (s32[1024]{0:T(1024)S(1)}, s32[1024]{0:T(1024)}, u32[]{:S(2)}) copy-start(s32[1024]{0:T(1024)} %get-tuple-element.225) | copy-start | bytes 12292
  184.4 36.6 %collective-permute-start.21 = (bf16[256,1024]{0,1:T(8,128)(2,1)}, bf16[256,1024]{0,1:T(8,128)(2,1)}, u32[]{:S(2)}, u32[]{:S(2)}) collective-permute-start(bf16[256,1024]{0,1:T(8,128)(2,1)} %get-tuple-element.18), channel_id=1, source_target_pairs={{0,4},{1,5},{2,6},{3,7},{4,0},{5,1},{6,2},{7,3},{8,12},{9,13},{10,... | collective-permute-start | bytes 1572872 | tf_op jit(solution)/shard_map/ppermute | solution.py:20
  209.4 188.5 %copy-start.17 = (pred[1024]{0:T(1024)(128)(4,1)S(1)}, pred[1024]{0:T(1024)(128)(4,1)}, u32[]{:S(2)}) copy-start(pred[1024]{0:T(1024)(128)(4,1)} %copy-done.16) | copy-start | bytes 3076
  209.4 61.6 %collective-permute-start.15 = (f32[256,1024]{0,1:T(8,128)}, f32[256,1024]{0,1:T(8,128)}, u32[]{:S(2)}, u32[]{:S(2)}) collective-permute-start(f32[256,1024]{0,1:T(8,128)} %fusion.3), channel_id=1, source_target_pairs={{0,8},{1,9},{2,10},{3,11},{4,12},{5,13},{6,14},{7,15},{8,0},{9,1},... | collective-permute-start | bytes 3145736 | tf_op jit(solution)/shard_map/ppermute | solution.py:20
  223.2 47.7 %collective-permute-start.22 = (bf16[256,1024]{0,1:T(8,128)(2,1)}, bf16[256,1024]{0,1:T(8,128)(2,1)}, u32[]{:S(2)}, u32[]{:S(2)}) collective-permute-start(bf16[256,1024]{0,1:T(8,128)(2,1)} %fusion.57), channel_id=1, source_target_pairs={{0,8},{1,9},{2,10},{3,11},{4,12},{5,13},{6,14},{7,15},{8,0},{9,1},... | collective-permute-start | bytes 1572872 | tf_op jit(solution)/shard_map/ppermute | solution.py:20
  270.9 129.2 %copy-start.13 = (pred[1024]{0:T(1024)(128)(4,1)S(1)}, pred[1024]{0:T(1024)(128)(4,1)}, u32[]{:S(2)}) copy-start(pred[1024]{0:T(1024)(128)(4,1)} %copy-done.12) | copy-start | bytes 3076
  273.7 61.2 %collective-permute-start.16 = (f32[256,1024]{0,1:T(8,128)S(1)}, f32[256,1024]{0,1:T(8,128)S(1)}, u32[]{:S(2)}, u32[]{:S(2)}) collective-permute-start(f32[256,1024]{0,1:T(8,128)S(1)} %get-tuple-element.17), channel_id=1, source_target_pairs={{0,4},{1,5},{2,6},{3,7},{4,0},{5,1},{6,2},{7,3},{8,12},{9,13},{10,... | collective-permute-start | bytes 3145736 | tf_op jit(solution)/shard_map/ppermute | solution.py:20
  335.2 24.3 %collective-permute-start.17 = (f32[256,1024]{0,1:T(8,128)S(1)}, f32[256,1024]{0,1:T(8,128)S(1)}, u32[]{:S(2)}, u32[]{:S(2)}) collective-permute-start(f32[256,1024]{0,1:T(8,128)S(1)} %multiply_subtract_fusion.11), channel_id=1, source_target_pairs={{0,2},{1,3},{2,0},{3,1},{4,6},{5,7},{6,4},{7,5},{8,10},{9,11},{10,... | collective-permute-start | bytes 3145736 | tf_op jit(solution)/shard_map/ppermute | solution.py:20
  361.6 33.4 %collective-permute-start.18 = (f32[256,1024]{0,1:T(8,128)}, f32[256,1024]{0,1:T(8,128)S(1)}, u32[]{:S(2)}, u32[]{:S(2)}) collective-permute-start(f32[256,1024]{0,1:T(8,128)} %get-tuple-element.20), channel_id=1, source_target_pairs={{0,1},{1,0},{2,3},{3,2},{4,5},{5,4},{6,7},{7,6},{8,9},{9,8},{10,11... | collective-permute-start | bytes 3145736 | tf_op jit(solution)/shard_map/ppermute | solution.py:20
  397.6 5.8 %copy-start.11 = (pred[1024]{0:T(1024)(128)(4,1)S(1)}, pred[1024]{0:T(1024)(128)(4,1)}, u32[]{:S(2)}) copy-start(pred[1024]{0:T(1024)(128)(4,1)} %copy-done.10) | copy-start | bytes 3076
  399.9 6.6 %copy-start.9 = (pred[1024]{0:T(1024)(128)(4,1)S(1)}, pred[1024]{0:T(1024)(128)(4,1)}, u32[]{:S(2)}) copy-start(pred[1024]{0:T(1024)(128)(4,1)} %copy-done.8) | copy-start | bytes 3076
  403.2 6.3 %copy-start.7 = (pred[1024]{0:T(1024)(128)(4,1)S(1)}, pred[1024]{0:T(1024)(128)(4,1)}, u32[]{:S(2)}) copy-start(pred[1024]{0:T(1024)(128)(4,1)} %copy-done.6) | copy-start | bytes 3076
  406.3 6.1 %copy-start.5 = (pred[1024]{0:T(1024)(128)(4,1)S(1)}, pred[1024]{0:T(1024)(128)(4,1)}, u32[]{:S(2)}) copy-start(pred[1024]{0:T(1024)(128)(4,1)} %copy-done.4) | copy-start | bytes 3076
  409.3 6.0 %copy-start.3 = (pred[1024]{0:T(1024)(128)(4,1)S(1)}, pred[1024]{0:T(1024)(128)(4,1)}, u32[]{:S(2)}) copy-start(pred[1024]{0:T(1024)(128)(4,1)} %copy-done.2) | copy-start | bytes 3076
  412.3 6.1 %copy-start.15 = (pred[1024]{0:T(1024)(128)(4,1)S(1)}, pred[1024]{0:T(1024)(128)(4,1)}, u32[]{:S(2)}) copy-start(pred[1024]{0:T(1024)(128)(4,1)} %copy-done.14) | copy-start | bytes 3076
  509.9 21.4 %all-to-all-start = ((f32[16,14,512]{2,1,0:T(8,128)}), f32[16,14,512]{2,1,0:T(8,128)}, u32[]{:S(2)}, u32[]{:S(2)}) async-start(f32[16,14,512]{2,1,0:T(8,128)} %bitcast.44), calls=%async_computation | async-start | bytes 1048576 | tf_op jit(solution)/shard_map/all_to_all | solution.py:31
  533.3 16.3 %all-to-all-start.1 = ((f32[16,14,512]{2,1,0:T(8,128)}), f32[16,14,512]{2,1,0:T(8,128)}, u32[]{:S(2)}, u32[]{:S(2)}) async-start(f32[16,14,512]{2,1,0:T(8,128)} %broadcast_in_dim.368), calls=%async_computation.1 | async-start | bytes 1048576 | tf_op jit(solution)/shard_map/all_to_all | solution.py:37
Sparse Core Ops, SparseCore 0:
  9.8 49.3 all-gather.4
  61.6 135.1 all-gather.2
